TPU v7x, 32 devices: a whole 2x2x4 slice. The times are simulated.
32 devices in a mesh: pairs: 2 (over x), tgt: 16 (over z, y, core).
Axes of the slice: x: 2, y: 2, z: 4, core: 2. Of those that a mesh axis runs over, the one named last changes fastest.
Arguments:
- src_hidden: bfloat16 [4096, 128], P(('pairs', 'tgt')), parts along dimension 0, may hold values from -6 to 6
- tgt_hidden: bfloat16 [256, 256, 128], P(('pairs', 'tgt')), parts along dimension 0, may hold values from -6 to 6
- proj_weight: bfloat16 [128, 256], replicated, may hold values from -0.5 to 0.5
- proj_bias: float32 [256], replicated, may hold values from -1.5 to 1.5
Outputs:
- level_one: bfloat16 [128, 128, 2048], P(('pairs', 'tgt')), parts along dimension 0
- level_two: bfloat16 [4096, 2048], P(('pairs', 'tgt')), parts along dimension 0
- level_three: bfloat16 [4096, 512], P(('pairs', 'tgt')), parts along dimension 0
There are 2 independent parts, one for each index of `pairs`. A program takes and returns all parts, laid end to end along the dimension named above; an argument that names none is the same for every part. Nothing has to cross between parts.
All inputs are finite; a program needn't handle non-finite values.
Results may differ from a plain program's by a relative error of at most 0.006.
Values may be sent and summed in bfloat16 or wider, within the bound.
A program may use at most 64 MiB of HBM per device.

v0:
```python
import math
import jax
import jax.numpy as jnp
from jax import lax
from jax.sharding import PartitionSpec as P


def project_features(hidden, weight, bias):
    result = jnp.dot(hidden, weight, preferred_element_type=jnp.float32) + bias
    return result.astype(jnp.bfloat16)


def pool_leading(values):
    height, across, depth = values.shape
    return values.reshape(height // 2, 2, across // 2, 2, depth).mean(axis=(1, 3))


def pool_trailing(values):
    depth, height, across = values.shape
    return values.reshape(depth, height // 2, 2, across // 2, 2).mean(axis=(2, 4))


def split_parts(values):
    upper = values.astype(jnp.bfloat16)
    lower = (values - upper.astype(jnp.float32)).astype(jnp.bfloat16)
    return (upper, lower)


def per_device(src_hidden, tgt_hidden, proj_weight, proj_bias):
    row_count, col_count, hidden_width = tgt_hidden.shape
    channels = proj_weight.shape[1]
    stripe_count = lax.axis_size("tgt")
    own_sources = src_hidden.shape[0]
    source_count = own_sources * stripe_count
    inverse_root = 1.0 / math.sqrt(channels)
    tgt_feat = project_features(
        tgt_hidden.reshape(row_count * col_count, hidden_width), proj_weight, proj_bias
    )
    grid_feat = tgt_feat.astype(jnp.float32).reshape(row_count, col_count, channels)
    fine_pool = pool_leading(grid_feat)
    coarse_pool = pool_leading(fine_pool)
    fine_upper, fine_lower = split_parts(fine_pool.reshape(-1, channels))
    coarse_upper, coarse_lower = split_parts(coarse_pool.reshape(-1, channels))
    own_features = project_features(src_hidden, proj_weight, proj_bias)
    all_features = lax.all_gather(own_features, "tgt", axis=0, tiled=True)
    block_size = 512
    block_total = source_count // block_size
    fine_count = fine_upper.shape[0]
    coarse_count = coarse_upper.shape[0]
    empty_levels = (
        jnp.zeros((fine_count, source_count), jnp.bfloat16),
        jnp.zeros((source_count, coarse_count), jnp.bfloat16),
    )
    contract_last = (((1,), (1,)), ((), ()))

    def one_block(block_index, levels):
        level_one, coarse_rows = levels
        offset = (block_index * block_size).astype(jnp.int32)
        panel = lax.dynamic_slice_in_dim(all_features, offset, block_size, 0)
        fine_corr = lax.dot_general(
            fine_upper, panel, contract_last, preferred_element_type=jnp.float32
        )
        fine_corr = fine_corr + lax.dot_general(
            fine_lower, panel, contract_last, preferred_element_type=jnp.float32
        )
        coarse_corr = lax.dot_general(
            panel, coarse_upper, contract_last, preferred_element_type=jnp.float32
        )
        coarse_corr = coarse_corr + lax.dot_general(
            panel, coarse_lower, contract_last, preferred_element_type=jnp.float32
        )
        zero_index = jnp.zeros((), jnp.int32)
        level_one = lax.dynamic_update_slice(
            level_one, (fine_corr * inverse_root).astype(jnp.bfloat16), (zero_index, offset)
        )
        coarse_rows = lax.dynamic_update_slice(
            coarse_rows, (coarse_corr * inverse_root).astype(jnp.bfloat16), (offset, zero_index)
        )
        return (level_one, coarse_rows)

    level_one, coarse_rows = lax.fori_loop(0, block_total, one_block, empty_levels)
    level_one = level_one.reshape(row_count // 2, col_count // 2, source_count)
    level_two = lax.all_to_all(coarse_rows, "tgt", split_axis=0, concat_axis=1, tiled=True)
    coarse_grid = level_two.astype(jnp.float32).reshape(
        own_sources, stripe_count * (row_count // 4), col_count // 4
    )
    level_three = pool_trailing(coarse_grid).reshape(own_sources, -1).astype(jnp.bfloat16)
    return (level_one, level_two, level_three)


def solution(mesh):
    return jax.shard_map(
        per_device,
        mesh=mesh,
        in_specs=(P(("pairs", "tgt"), None), P(("pairs", "tgt"), None, None), P(), P()),
        out_specs=(
            P(("pairs", "tgt"), None, None),
            P(("pairs", "tgt"), None),
            P(("pairs", "tgt"), None),
        ),
        check_vma=False,
    )
```

profile of v0, /device:TPU:0, one launch (start us, length us, event | category | flops | bytes accessed | tf_op | source)
XLA Modules:
  0.0 93.0 jit_solution(4818545377180773034)
XLA Ops:
  7.2 0.0 copy-start
  7.2 0.0 all-gather.2.cloned.1.call-start
  7.2 1.7 %fusion.18 = bf16[128,256]{1,0:T(8,128)(2,1)} fusion(bf16[128,128]{1,0:T(8,128)(2,1)} %param.6, bf16[128,256]{1,0:T(8,128)(2,1)} %param.8, f32[256]{0:T(256)} %param.9), kind=kOutput, calls=%fused_computation.23 | convolution fusion | flops 8454144 | bytes 164864 | tf_op jit(solution)/shard_map/dot_general | solution.py:9
  8.9 0.0 all-gather.2.cloned.1.call-update
  8.9 0.0 copy-done
  8.9 2.6 %fusion.17 = f32[2048,256]{1,0:T(8,128)} fusion(bf16[2048,128]{1,0:T(8,128)(2,1)S(1)} %bitcast.40, bf16[128,256]{1,0:T(8,128)(2,1)} %param.8, f32[256]{0:T(256)} %param.9), kind=kOutput, calls=%fused_computation.21 | convolution fusion | flops 135790592 | bytes 2688000 | tf_op jit(solution)/shard_map/dot_general | solution.py:9
  11.5 2.5 %reshape.38 = f32[4,2,128,2,256]{4,3,2,1,0:T(2,128)S(1)} reshape(f32[2048,256]{1,0:T(8,128)} %fusion.17) | data formatting | bytes 4194304 | tf_op jit(solution)/shard_map/reshape;reshape | solution.py:15
  14.0 1.5 %reduce_sum.27 = f32[4,128,256]{2,1,0:T(8,128)S(1)} reduce(f32[4,2,128,2,256]{4,3,2,1,0:T(2,128)S(1)} %reshape.38, f32[]{:T(128)} %constant.47.clone.1), dimensions={1,3}, to_apply=%region_0.0 | reduce | flops 393216 | bytes 2621444 | tf_op jit(solution)/shard_map/reduce_sum | solution.py:15
  15.5 0.3 div.27
  15.9 0.4 reduce_sum.28
  16.3 35.1 %all-gather.2.cloned.1.call-done = bf16[2048,256]{1,0:T(8,128)(2,1)} async-done(((bf16[128,256]{1,0:T(8,128)(2,1)}), bf16[2048,256]{1,0:T(8,128)(2,1)}) %all-gather.2.cloned.1.call-update) | async-done | bytes 1048592 | tf_op jit(solution)/shard_map/all_gather | solution.py:45
  51.4 0.0 copy-start.1
  51.4 0.9 broadcast_in_dim.9
  52.3 1.6 %broadcast_in_dim.8.clone = bf16[512,2048]{1,0:T(8,128)(2,1)} broadcast(bf16[]{:T(256)} %constant.46.clone.1), dimensions={} | broadcast | bytes 2097154 | tf_op jit(solution)/shard_map/broadcast_in_dim | solution.py:51
  53.9 0.0 copy-done.1
  53.9 11.4 %while.15 = (s32[]{:T(128)}, bf16[512,2048]{1,0:T(8,128)(2,1)}, bf16[2048,128]{1,0:T(8,128)(2,1)}, bf16[2048,256]{1,0:T(8,128)(2,1)S(1)}, bf16[512,256]{1,0:T(8,...) while((s32[]{:T(128)}, bf16[512,2048]{1,0:T(8,128)(2,1)}, ...), condition=%wide.region_3.0_spmd, body=%wide.region_2.0_spmd.sunk | while | flops 336527360 | bytes 7079091 | solution.py:81
  53.9 0.2 fusion.51
  54.1 0.9 fusion.52
  55.0 0.3 fusion.49
  55.3 0.3 fusion.50
  55.7 0.2 copy.30
  55.9 0.8 constant_dynamic-update-slice_fusion.2
  56.7 0.2 fusion.51
  56.9 0.9 fusion.52
  57.8 0.3 fusion.49
  58.2 0.3 fusion.50
  58.5 0.2 copy.30
  58.7 0.8 constant_dynamic-update-slice_fusion.2
  59.5 0.2 fusion.51
  59.8 0.9 fusion.52
  60.7 0.3 fusion.49
  61.0 0.3 fusion.50
  61.3 0.2 copy.30
  61.5 0.8 constant_dynamic-update-slice_fusion.2
  62.4 0.2 fusion.51
  62.6 0.9 fusion.52
  63.5 0.3 fusion.49
  63.8 0.3 fusion.50
  64.2 0.2 copy.30
  64.4 0.8 constant_dynamic-update-slice_fusion.2
  65.2 18.1 %all_to_all.19 = bf16[16,128,128]{2,1,0:T(8,128)(2,1)S(1)} all-to-all(bf16[16,128,128]{2,1,0:T(8,128)(2,1)} %bitcast.5), channel_id=1, replica_groups=mesh['pairs'=2,'tgt'=16] {'tgt'}, dimensions={0} | all-to-all | bytes 1048576 | tf_op jit(solution)/shard_map/all_to_all | solution.py:83
  83.3 0.3 copy.22
  83.6 1.0 %copy.25 = bf16[128,2048]{1,0:T(8,128)(2,1)} copy(bf16[128,2048]{0,1:T(8,128)(2,1)S(1)} %bitcast.44) | data formatting | bytes 1048576
  84.6 0.1 bitcast_convert_fusion.2
  84.7 0.5 copy.23
  85.2 0.1 reduce_sum.29
  85.4 0.8 copy.26
  (6 shorter events, 0.2 us)
Async XLA Ops:
  7.2 1.8 %copy-start = (bf16[8,256,128]{2,1,0:T(8,128)(2,1)S(1)}, bf16[8,256,128]{2,1,0:T(8,128)(2,1)}, u32[]{:S(2)}) copy-start(bf16[8,256,128]{2,1,0:T(8,128)(2,1)} %param.7) | copy-start | bytes 1572868
  7.2 44.2 %all-gather.2.cloned.1.call-start = ((), (), s32[]{:S(2)}) async-start(), calls=%async_computation.1 | async-start | bytes 1114112 | tf_op jit(solution)/shard_map/all_gather | solution.py:45
  51.4 2.4 %copy-start.1 = (bf16[2048,256]{1,0:T(8,128)(2,1)S(1)}, bf16[2048,256]{1,0:T(8,128)(2,1)}, u32[]{:S(2)}) copy-start(bf16[2048,256]{1,0:T(8,128)(2,1)} %all-gather.2.cloned.1.call-done) | copy-start | bytes 3145732
Sparse Core Ops, SparseCore 0:
  10.8 40.6 all-gather.1
where the time goes:
time: 93.3 us; the launch traced here: 93 us
  waiting for transfers between devices  35.1 us (38%)
  blocking collectives  18.1 us (19%)
  between operations  14.2 us (15%)
  local copies, waits for them, and re-layouts  12 us (13%)
  matrix products  11.3 us (12%)
  other arithmetic  2.17 us (2%)
    all_gather x1, waiting for transfers between devices, per_device(): all_features = lax.all_gather(own_features, 'tgt', axis=0, tiled=True)  35.1 us
    all_to_all x1, blocking collectives, per_device(): lax.all_to_all(coarse_rows, 'tgt', split_axis=0, concat_axis=1, tiled=True)  18.1 us
    dot_general x2, matrix products, project_features(): result = jnp.dot(hidden, weight, preferred_element_type=jnp.float32) + bias  4.25 us
    dynamic_update_slice x8, local copies, waits for them, and re-layouts, one_block(): lax.dynamic_update_slice(level_one, (fine_corr * inverse_root).astype(jnp...  4.19 us
    dot_general x4, matrix products, one_block(): lax.dot_general(panel, coarse_lower, contract_last, preferred_element_typ...  3.57 us
    another operation x1, local copies, waits for them, and re-layouts, pool_leading(): values.reshape(height // 2, 2, across // 2, 2, depth).mean(axis=(1, 3))  2.49 us
  transfers between devices with their start and end apart: 1, of which 1 were waited for; matrix products, arithmetic and copies ran while one was open for 8% of the time, Pallas kernels for 0%

commit v1 on v0

--- a/solution.py
+++ b/solution.py
@@ -42,7 +42,17 @@
     fine_upper, fine_lower = split_parts(fine_pool.reshape(-1, channels))
     coarse_upper, coarse_lower = split_parts(coarse_pool.reshape(-1, channels))
     own_features = project_features(src_hidden, proj_weight, proj_bias)
-    all_features = lax.all_gather(own_features, "tgt", axis=0, tiled=True)
+    count, index, extent = (lax.axis_size("tgt"), lax.axis_index("tgt"), own_features.shape[0])
+    right = [(i, (i + 1) % count) for i in range(count)]
+    all_features = jnp.zeros(
+        (*own_features.shape[:0], count * extent, *own_features.shape[0 + 1 :]), own_features.dtype
+    )
+    held = own_features
+    for step in range(count):
+        holder = (index - step) % count
+        all_features = lax.dynamic_update_slice_in_dim(all_features, held, holder * extent, axis=0)
+        if step < count - 1:
+            held = lax.ppermute(held, "tgt", right)
     block_size = 512
     block_total = source_count // block_size
     fine_count = fine_upper.shape[0]

time: 93.3 us -> 138 us (1.48)
  waiting for transfers between devices: 35.1 us -> 87.2 us
  between operations: 14.2 us -> 1.17 us
  starting transfers between devices: 0.04 us -> 3.23 us
  other arithmetic: 2.17 us -> 3.79 us
    ppermute x0 -> x15, waiting for transfers between devices: none -> 87.2 us  [per_device(): held = lax.ppermute(held, 'tgt', right)]
    all_gather x1 -> x0, waiting for transfers between devices: 35.1 us -> none  [per_device(): all_features = lax.all_gather(own_features, 'tgt', axis=0, tiled=True)]
    ppermute x0 -> x15, starting transfers between devices: none -> 3.23 us  [per_device(): held = lax.ppermute(held, 'tgt', right)]
    reduce_sum x2, other arithmetic: 1.84 us -> 3.46 us  [pool_leading(): values.reshape(height // 2, 2, across // 2, 2, depth).mean(axis=(1, 3))]
  transfers between devices with their start and end apart: 1 -> 15, of which waited for: 1 -> 14; matrix products, arithmetic and copies ran while one was open for 8% -> 7% of each run, Pallas kernels for 0% -> 0%
where the time goes in v1:
time: 138 us; the launch traced here: 137 us
  waiting for transfers between devices  87.2 us (63%)
  blocking collectives  18 us (13%)
  local copies, waits for them, and re-layouts  13.2 us (10%)
  matrix products  10.7 us (8%)
  other arithmetic  3.79 us (3%)
  starting transfers between devices  3.23 us (2%)
    ppermute x15, waiting for transfers between devices, per_device(): held = lax.ppermute(held, 'tgt', right)  87.2 us
    all_to_all x1, blocking collectives, per_device(): lax.all_to_all(coarse_rows, 'tgt', split_axis=0, concat_axis=1, tiled=True)  18 us
    dynamic_update_slice x8, local copies, waits for them, and re-layouts, one_block(): lax.dynamic_update_slice(level_one, (fine_corr * inverse_root).astype(jnp...  4.19 us
    dot_general x2, matrix products, project_features(): result = jnp.dot(hidden, weight, preferred_element_type=jnp.float32) + bias  3.61 us
    dot_general x4, matrix products, one_block(): lax.dot_general(panel, coarse_lower, contract_last, preferred_element_typ...  3.56 us
    another operation x1, local copies, waits for them, and re-layouts, pool_leading(): values.reshape(height // 2, 2, across // 2, 2, depth).mean(axis=(1, 3))  3.47 us
    reduce_sum x2, other arithmetic, pool_leading(): values.reshape(height // 2, 2, across // 2, 2, depth).mean(axis=(1, 3))  3.46 us
    ppermute x15, starting transfers between devices, per_device(): held = lax.ppermute(held, 'tgt', right)  3.23 us
  transfers between devices with their start and end apart: 15, of which 14 were waited for; matrix products, arithmetic and copies ran while one was open for 7% of the time, Pallas kernels for 0%

profile of v1, /device:TPU:0, one launch (start us, length us, event | category | flops | bytes accessed | tf_op | source)
XLA Modules:
  0.0 137.3 jit_solution(17632366642363668602)
XLA Ops:
  0.7 1.0 constant_dynamic-update-slice_fusion.16
  1.8 0.5 collective-permute-start
  2.3 2.6 %fusion.17 = f32[2048,256]{1,0:T(8,128)} fusion(bf16[2048,128]{1,0:T(8,128)(2,1)S(1)} %bitcast.40, bf16[128,256]{1,0:T(8,128)(2,1)} %param.8, f32[256]{0:T(256)} %param.9), kind=kOutput, calls=%fused_computation.21 | convolution fusion | flops 135790592 | bytes 2688000 | tf_op jit(solution)/shard_map/dot_general | solution.py:9
  4.9 3.5 %reshape.38 = f32[4,2,128,2,256]{4,3,2,1,0:T(2,128)} reshape(f32[2048,256]{1,0:T(8,128)} %fusion.17) | data formatting | bytes 4194304 | tf_op jit(solution)/shard_map/reshape;reshape | solution.py:15
  8.3 3.1 %reduce_sum.27 = f32[4,128,256]{2,1,0:T(8,128)S(1)} reduce(f32[4,2,128,2,256]{4,3,2,1,0:T(2,128)} %reshape.38, f32[]{:T(128)} %constant.173.clone.1), dimensions={1,3}, to_apply=%region_0.0 | reduce | flops 393216 | bytes 2621444 | tf_op jit(solution)/shard_map/reduce_sum | solution.py:15
  11.5 0.3 div.27
  11.9 0.4 reduce_sum.28
  12.6 2.7 %collective-permute-start.1 = (bf16[128,256]{1,0:T(8,128)(2,1)S(1)}, bf16[128,256]{1,0:T(8,128)(2,1)S(1)}, u32[]{:S(2)}, u32[]{:S(2)}) collective-permute-start(bf16[128,256]{1,0:T(8,128)(2,1)S(1)} %collective-permute-done), channel_id=1, source_target_pairs={{0,1},{1,2},{2,3},{3,4},{4,5},{5,6},{6,7},{7,8},{8,9},{9,10},{10,1... | collective-permute-start | bytes 196616 | tf_op jit(solution)/shard_map/ppermute | solution.py:55
  15.3 4.3 %collective-permute-done.1 = bf16[128,256]{1,0:T(8,128)(2,1)S(1)} collective-permute-done((bf16[128,256]{1,0:T(8,128)(2,1)S(1)}, bf16[128,256]{1,0:T(8,128)(2,1)S(1)}, u32[]{:S(2)}, u32[]{:S(2)}) %collective-permute-start.1) | collective-permute-done | bytes 65568 | tf_op jit(solution)/shard_map/ppermute | solution.py:55
  19.7 6.4 %collective-permute-done.2 = bf16[128,256]{1,0:T(8,128)(2,1)S(1)} collective-permute-done((bf16[128,256]{1,0:T(8,128)(2,1)S(1)}, bf16[128,256]{1,0:T(8,128)(2,1)S(1)}, u32[]{:S(2)}, u32[]{:S(2)}) %collective-permute-start.2) | collective-permute-done | bytes 65568 | tf_op jit(solution)/shard_map/ppermute | solution.py:55
  26.0 6.4 %collective-permute-done.3 = bf16[128,256]{1,0:T(8,128)(2,1)S(1)} collective-permute-done((bf16[128,256]{1,0:T(8,128)(2,1)S(1)}, bf16[128,256]{1,0:T(8,128)(2,1)S(1)}, u32[]{:S(2)}, u32[]{:S(2)}) %collective-permute-start.3) | collective-permute-done | bytes 65568 | tf_op jit(solution)/shard_map/ppermute | solution.py:55
  32.4 6.4 %collective-permute-done.4 = bf16[128,256]{1,0:T(8,128)(2,1)S(1)} collective-permute-done((bf16[128,256]{1,0:T(8,128)(2,1)S(1)}, bf16[128,256]{1,0:T(8,128)(2,1)S(1)}, u32[]{:S(2)}, u32[]{:S(2)}) %collective-permute-start.4) | collective-permute-done | bytes 65568 | tf_op jit(solution)/shard_map/ppermute | solution.py:55
  38.8 6.4 %collective-permute-done.5 = bf16[128,256]{1,0:T(8,128)(2,1)S(1)} collective-permute-done((bf16[128,256]{1,0:T(8,128)(2,1)S(1)}, bf16[128,256]{1,0:T(8,128)(2,1)S(1)}, u32[]{:S(2)}, u32[]{:S(2)}) %collective-permute-start.5) | collective-permute-done | bytes 65568 | tf_op jit(solution)/shard_map/ppermute | solution.py:55
  45.2 6.4 %collective-permute-done.6 = bf16[128,256]{1,0:T(8,128)(2,1)S(1)} collective-permute-done((bf16[128,256]{1,0:T(8,128)(2,1)S(1)}, bf16[128,256]{1,0:T(8,128)(2,1)S(1)}, u32[]{:S(2)}, u32[]{:S(2)}) %collective-permute-start.6) | collective-permute-done | bytes 65568 | tf_op jit(solution)/shard_map/ppermute | solution.py:55
  51.6 6.4 %collective-permute-done.7 = bf16[128,256]{1,0:T(8,128)(2,1)S(1)} collective-permute-done((bf16[128,256]{1,0:T(8,128)(2,1)S(1)}, bf16[128,256]{1,0:T(8,128)(2,1)S(1)}, u32[]{:S(2)}, u32[]{:S(2)}) %collective-permute-start.7) | collective-permute-done | bytes 65568 | tf_op jit(solution)/shard_map/ppermute | solution.py:55
  58.0 6.4 %collective-permute-done.8 = bf16[128,256]{1,0:T(8,128)(2,1)S(1)} collective-permute-done((bf16[128,256]{1,0:T(8,128)(2,1)S(1)}, bf16[128,256]{1,0:T(8,128)(2,1)S(1)}, u32[]{:S(2)}, u32[]{:S(2)}) %collective-permute-start.8) | collective-permute-done | bytes 65568 | tf_op jit(solution)/shard_map/ppermute | solution.py:55
  64.4 6.4 %collective-permute-done.9 = bf16[128,256]{1,0:T(8,128)(2,1)S(1)} collective-permute-done((bf16[128,256]{1,0:T(8,128)(2,1)S(1)}, bf16[128,256]{1,0:T(8,128)(2,1)S(1)}, u32[]{:S(2)}, u32[]{:S(2)}) %collective-permute-start.9) | collective-permute-done | bytes 65568 | tf_op jit(solution)/shard_map/ppermute | solution.py:55
  70.8 6.4 %collective-permute-done.10 = bf16[128,256]{1,0:T(8,128)(2,1)S(1)} collective-permute-done((bf16[128,256]{1,0:T(8,128)(2,1)S(1)}, bf16[128,256]{1,0:T(8,128)(2,1)S(1)}, u32[]{:S(2)}, u32[]{:S(2)}) %collective-permute-start.10) | collective-permute-done | bytes 65568 | tf_op jit(solution)/shard_map/ppermute | solution.py:55
  77.1 6.4 %collective-permute-done.11 = bf16[128,256]{1,0:T(8,128)(2,1)S(1)} collective-permute-done((bf16[128,256]{1,0:T(8,128)(2,1)S(1)}, bf16[128,256]{1,0:T(8,128)(2,1)S(1)}, u32[]{:S(2)}, u32[]{:S(2)}) %collective-permute-start.11) | collective-permute-done | bytes 65568 | tf_op jit(solution)/shard_map/ppermute | solution.py:55
  83.5 6.4 %collective-permute-done.12 = bf16[128,256]{1,0:T(8,128)(2,1)S(1)} collective-permute-done((bf16[128,256]{1,0:T(8,128)(2,1)S(1)}, bf16[128,256]{1,0:T(8,128)(2,1)S(1)}, u32[]{:S(2)}, u32[]{:S(2)}) %collective-permute-start.12) | collective-permute-done | bytes 65568 | tf_op jit(solution)/shard_map/ppermute | solution.py:55
  89.9 6.4 %collective-permute-done.13 = bf16[128,256]{1,0:T(8,128)(2,1)S(1)} collective-permute-done((bf16[128,256]{1,0:T(8,128)(2,1)S(1)}, bf16[128,256]{1,0:T(8,128)(2,1)S(1)}, u32[]{:S(2)}, u32[]{:S(2)}) %collective-permute-start.13) | collective-permute-done | bytes 65568 | tf_op jit(solution)/shard_map/ppermute | solution.py:55
  96.3 6.4 %collective-permute-done.14 = bf16[128,256]{1,0:T(8,128)(2,1)S(1)} collective-permute-done((bf16[128,256]{1,0:T(8,128)(2,1)S(1)}, bf16[128,256]{1,0:T(8,128)(2,1)S(1)}, u32[]{:S(2)}, u32[]{:S(2)}) %collective-permute-start.14) | collective-permute-done | bytes 65568 | tf_op jit(solution)/shard_map/ppermute | solution.py:55
  102.7 0.9 broadcast_in_dim.12
  103.6 1.6 %broadcast_in_dim.11.clone = bf16[512,2048]{1,0:T(8,128)(2,1)} broadcast(bf16[]{:T(256)} %constant.152.clone.1), dimensions={} | broadcast | bytes 2097154 | tf_op jit(solution)/shard_map/broadcast_in_dim | solution.py:61
  105.1 11.4 %while.15 = (s32[]{:T(128)}, bf16[512,2048]{1,0:T(8,128)(2,1)}, bf16[2048,128]{1,0:T(8,128)(2,1)}, bf16[2048,256]{1,0:T(8,128)(2,1)S(1)}, bf16[512,256]{1,0:T(8,...) while((s32[]{:T(128)}, bf16[512,2048]{1,0:T(8,128)(2,1)}, ...), condition=%wide.region_3.4_spmd, body=%wide.region_2.3_spmd.sunk | while | flops 336527360 | bytes 7079091 | solution.py:91
  105.4 0.9 fusion.52
  106.2 0.3 fusion.49
  106.6 0.3 fusion.50
  107.1 0.8 constant_dynamic-update-slice_fusion.18
  108.0 0.2 fusion.51
  108.2 0.9 fusion.52
  109.1 0.3 fusion.49
  109.4 0.3 fusion.50
  110.0 0.8 constant_dynamic-update-slice_fusion.18
  110.8 0.2 fusion.51
  111.0 0.9 fusion.52
  111.9 0.3 fusion.49
  112.3 0.3 fusion.50
  112.8 0.8 constant_dynamic-update-slice_fusion.18
  113.9 0.9 fusion.52
  114.8 0.3 fusion.49
  115.1 0.3 fusion.50
  115.7 0.8 constant_dynamic-update-slice_fusion.18
  116.5 18.0 %all_to_all.19 = bf16[16,128,128]{2,1,0:T(8,128)(2,1)S(1)} all-to-all(bf16[16,128,128]{2,1,0:T(8,128)(2,1)} %bitcast.5), channel_id=1, replica_groups=mesh['pairs'=2,'tgt'=16] {'tgt'}, dimensions={0} | all-to-all | bytes 1048576 | tf_op jit(solution)/shard_map/all_to_all | solution.py:93
  134.5 0.3 copy.22
  134.8 1.0 copy.25
  135.9 0.5 copy.23
  136.6 0.8 copy.26
  (46 shorter events, 1.9 us)
Async XLA Ops:
  0.6 1.7 %copy-start = (bf16[8,256,128]{2,1,0:T(8,128)(2,1)S(1)}, bf16[8,256,128]{2,1,0:T(8,128)(2,1)}, u32[]{:S(2)}) copy-start(bf16[8,256,128]{2,1,0:T(8,128)(2,1)} %param.7) | copy-start | bytes 1572868
  1.8 10.8 %collective-permute-start = (bf16[128,256]{1,0:T(8,128)(2,1)S(1)}, bf16[128,256]{1,0:T(8,128)(2,1)S(1)}, u32[]{:S(2)}, u32[]{:S(2)}) collective-permute-start(bf16[128,256]{1,0:T(8,128)(2,1)S(1)} %get-tuple-element.178), channel_id=1, source_target_pairs={{0,1},{1,2},{2,3},{3,4},{4,5},{5,6},{6,7},{7,8},{8,9},{9,10},{10,1... | collective-permute-start | bytes 196616 | tf_op jit(solution)/shard_map/ppermute | solution.py:55
  12.6 7.0 %collective-permute-start.1 = (bf16[128,256]{1,0:T(8,128)(2,1)S(1)}, bf16[128,256]{1,0:T(8,128)(2,1)S(1)}, u32[]{:S(2)}, u32[]{:S(2)}) collective-permute-start(bf16[128,256]{1,0:T(8,128)(2,1)S(1)} %collective-permute-done), channel_id=1, source_target_pairs={{0,1},{1,2},{2,3},{3,4},{4,5},{5,6},{6,7},{7,8},{8,9},{9,10},{10,1... | collective-permute-start | bytes 196616 | tf_op jit(solution)/shard_map/ppermute | solution.py:55
  19.6 6.4 %collective-permute-start.2 = (bf16[128,256]{1,0:T(8,128)(2,1)S(1)}, bf16[128,256]{1,0:T(8,128)(2,1)S(1)}, u32[]{:S(2)}, u32[]{:S(2)}) collective-permute-start(bf16[128,256]{1,0:T(8,128)(2,1)S(1)} %collective-permute-done.1), channel_id=1, source_target_pairs={{0,1},{1,2},{2,3},{3,4},{4,5},{5,6},{6,7},{7,8},{8,9},{9,10},{10,1... | collective-permute-start | bytes 196616 | tf_op jit(solution)/shard_map/ppermute | solution.py:55
  26.0 6.4 %collective-permute-start.3 = (bf16[128,256]{1,0:T(8,128)(2,1)S(1)}, bf16[128,256]{1,0:T(8,128)(2,1)S(1)}, u32[]{:S(2)}, u32[]{:S(2)}) collective-permute-start(bf16[128,256]{1,0:T(8,128)(2,1)S(1)} %collective-permute-done.2), channel_id=1, source_target_pairs={{0,1},{1,2},{2,3},{3,4},{4,5},{5,6},{6,7},{7,8},{8,9},{9,10},{10,1... | collective-permute-start | bytes 196616 | tf_op jit(solution)/shard_map/ppermute | solution.py:55
  32.4 6.4 %collective-permute-start.4 = (bf16[128,256]{1,0:T(8,128)(2,1)S(1)}, bf16[128,256]{1,0:T(8,128)(2,1)S(1)}, u32[]{:S(2)}, u32[]{:S(2)}) collective-permute-start(bf16[128,256]{1,0:T(8,128)(2,1)S(1)} %collective-permute-done.3), channel_id=1, source_target_pairs={{0,1},{1,2},{2,3},{3,4},{4,5},{5,6},{6,7},{7,8},{8,9},{9,10},{10,1... | collective-permute-start | bytes 196616 | tf_op jit(solution)/shard_map/ppermute | solution.py:55
  38.8 6.4 %collective-permute-start.5 = (bf16[128,256]{1,0:T(8,128)(2,1)S(1)}, bf16[128,256]{1,0:T(8,128)(2,1)S(1)}, u32[]{:S(2)}, u32[]{:S(2)}) collective-permute-start(bf16[128,256]{1,0:T(8,128)(2,1)S(1)} %collective-permute-done.4), channel_id=1, source_target_pairs={{0,1},{1,2},{2,3},{3,4},{4,5},{5,6},{6,7},{7,8},{8,9},{9,10},{10,1... | collective-permute-start | bytes 196616 | tf_op jit(solution)/shard_map/ppermute | solution.py:55
  45.2 6.4 %collective-permute-start.6 = (bf16[128,256]{1,0:T(8,128)(2,1)S(1)}, bf16[128,256]{1,0:T(8,128)(2,1)S(1)}, u32[]{:S(2)}, u32[]{:S(2)}) collective-permute-start(bf16[128,256]{1,0:T(8,128)(2,1)S(1)} %collective-permute-done.5), channel_id=1, source_target_pairs={{0,1},{1,2},{2,3},{3,4},{4,5},{5,6},{6,7},{7,8},{8,9},{9,10},{10,1... | collective-permute-start | bytes 196616 | tf_op jit(solution)/shard_map/ppermute | solution.py:55
  51.6 6.4 %collective-permute-start.7 = (bf16[128,256]{1,0:T(8,128)(2,1)S(1)}, bf16[128,256]{1,0:T(8,128)(2,1)S(1)}, u32[]{:S(2)}, u32[]{:S(2)}) collective-permute-start(bf16[128,256]{1,0:T(8,128)(2,1)S(1)} %collective-permute-done.6), channel_id=1, source_target_pairs={{0,1},{1,2},{2,3},{3,4},{4,5},{5,6},{6,7},{7,8},{8,9},{9,10},{10,1... | collective-permute-start | bytes 196616 | tf_op jit(solution)/shard_map/ppermute | solution.py:55
  58.0 6.4 %collective-permute-start.8 = (bf16[128,256]{1,0:T(8,128)(2,1)S(1)}, bf16[128,256]{1,0:T(8,128)(2,1)S(1)}, u32[]{:S(2)}, u32[]{:S(2)}) collective-permute-start(bf16[128,256]{1,0:T(8,128)(2,1)S(1)} %collective-permute-done.7), channel_id=1, source_target_pairs={{0,1},{1,2},{2,3},{3,4},{4,5},{5,6},{6,7},{7,8},{8,9},{9,10},{10,1... | collective-permute-start | bytes 196616 | tf_op jit(solution)/shard_map/ppermute | solution.py:55
  64.4 6.4 %collective-permute-start.9 = (bf16[128,256]{1,0:T(8,128)(2,1)S(1)}, bf16[128,256]{1,0:T(8,128)(2,1)S(1)}, u32[]{:S(2)}, u32[]{:S(2)}) collective-permute-start(bf16[128,256]{1,0:T(8,128)(2,1)S(1)} %collective-permute-done.8), channel_id=1, source_target_pairs={{0,1},{1,2},{2,3},{3,4},{4,5},{5,6},{6,7},{7,8},{8,9},{9,10},{10,1... | collective-permute-start | bytes 196616 | tf_op jit(solution)/shard_map/ppermute | solution.py:55
  70.7 6.4 %collective-permute-start.10 = (bf16[128,256]{1,0:T(8,128)(2,1)S(1)}, bf16[128,256]{1,0:T(8,128)(2,1)S(1)}, u32[]{:S(2)}, u32[]{:S(2)}) collective-permute-start(bf16[128,256]{1,0:T(8,128)(2,1)S(1)} %collective-permute-done.9), channel_id=1, source_target_pairs={{0,1},{1,2},{2,3},{3,4},{4,5},{5,6},{6,7},{7,8},{8,9},{9,10},{10,1... | collective-permute-start | bytes 196616 | tf_op jit(solution)/shard_map/ppermute | solution.py:55
  77.1 6.4 %collective-permute-start.11 = (bf16[128,256]{1,0:T(8,128)(2,1)S(1)}, bf16[128,256]{1,0:T(8,128)(2,1)S(1)}, u32[]{:S(2)}, u32[]{:S(2)}) collective-permute-start(bf16[128,256]{1,0:T(8,128)(2,1)S(1)} %collective-permute-done.10), channel_id=1, source_target_pairs={{0,1},{1,2},{2,3},{3,4},{4,5},{5,6},{6,7},{7,8},{8,9},{9,10},{10,1... | collective-permute-start | bytes 196616 | tf_op jit(solution)/shard_map/ppermute | solution.py:55
  83.5 6.4 %collective-permute-start.12 = (bf16[128,256]{1,0:T(8,128)(2,1)S(1)}, bf16[128,256]{1,0:T(8,128)(2,1)S(1)}, u32[]{:S(2)}, u32[]{:S(2)}) collective-permute-start(bf16[128,256]{1,0:T(8,128)(2,1)S(1)} %collective-permute-done.11), channel_id=1, source_target_pairs={{0,1},{1,2},{2,3},{3,4},{4,5},{5,6},{6,7},{7,8},{8,9},{9,10},{10,1... | collective-permute-start | bytes 196616 | tf_op jit(solution)/shard_map/ppermute | solution.py:55
  89.9 6.4 %collective-permute-start.13 = (bf16[128,256]{1,0:T(8,128)(2,1)S(1)}, bf16[128,256]{1,0:T(8,128)(2,1)S(1)}, u32[]{:S(2)}, u32[]{:S(2)}) collective-permute-start(bf16[128,256]{1,0:T(8,128)(2,1)S(1)} %collective-permute-done.12), channel_id=1, source_target_pairs={{0,1},{1,2},{2,3},{3,4},{4,5},{5,6},{6,7},{7,8},{8,9},{9,10},{10,1... | collective-permute-start | bytes 196616 | tf_op jit(solution)/shard_map/ppermute | solution.py:55
  96.3 6.4 %collective-permute-start.14 = (bf16[128,256]{1,0:T(8,128)(2,1)S(1)}, bf16[128,256]{1,0:T(8,128)(2,1)S(1)}, u32[]{:S(2)}, u32[]{:S(2)}) collective-permute-start(bf16[128,256]{1,0:T(8,128)(2,1)S(1)} %collective-permute-done.13), channel_id=1, source_target_pairs={{0,1},{1,2},{2,3},{3,4},{4,5},{5,6},{6,7},{7,8},{8,9},{9,10},{10,1... | collective-permute-start | bytes 196616 | tf_op jit(solution)/shard_map/ppermute | solution.py:55
